TPU v7x, 32 devices: a whole 2x2x4 slice. The times are simulated.
32 devices in a mesh: dp: 4 (over z), tensor: 4 (over y, x), section: 2 (over core).
Axes of the slice: x: 2, y: 2, z: 4, core: 2. Of those that a mesh axis runs over, the one named last changes fastest.
Arguments:
- grad_kv: bfloat16 [512, 2, 2, 1024], P('dp', 'section', None, 'tensor'), may hold values from -6 to 6
- kv_weight: bfloat16 [2, 2, 1024, 8192], P('section', None, 'tensor'), may hold values from -0.0625 to 0.0625
- image_count: int32 [32], P('dp'), may hold values from 1 to 2
- tile_count: int32 [32, 2], P('dp'), may hold values from 1 to 4, as said below
- image_owner: int32 [32, 2], P('dp'), may hold values from 0 to 3, as said below
- proj_weight: bfloat16 [8192, 1280], P(('tensor', 'section')), may hold values from -0.15625 to 0.15625
- vision_states: bfloat16 [512, 1280], P('dp'), may hold values from -60 to 60
- norm_gain: float32 [1280], replicated, may hold values from 0.5 to 2
Outputs:
- grad_vision: float32 [512, 1280], P(('dp', 'tensor', 'section'))
Inputs may be any that keep to these rules, and one draw needn't show every extreme that they name: `image_owner`: the 16 image slots of one decoder rank are shared evenly among the 4 owners, 4 slots each; live rows from one decoder rank to one owner number at most 32, and decoder rank 0 sends exactly 32 to owner 0. `tile_count`: some slots hold 4 tiles in every draw.
All inputs are finite; a program needn't handle non-finite values.
Results may differ from a plain program's by a relative error of at most 0.017.
Values may be sent and summed in bfloat16 or wider, within the bound.
A program may use at most 64 MiB of HBM per device.

v0:
```python
import jax
import jax.numpy as jnp
from jax import lax
from jax.sharding import PartitionSpec as P

TILE_TOK = 2


def per_device(
    grad_kv, kv_weight, image_count, tile_count, image_owner, proj_weight, vision_states, norm_gain
):
    tok_rows = grad_kv.shape[0]
    head_cols = grad_kv.shape[3]
    left_side = grad_kv.reshape(tok_rows, 2 * head_cols)
    right_side = kv_weight.reshape(2 * head_cols, kv_weight.shape[3])
    col_groups = lax.axis_size("tensor") * lax.axis_size("section")
    col_block = right_side.shape[1] // col_groups
    group_index = lax.axis_index(("tensor", "section"))
    partial_value = jnp.dot(left_side, right_side, preferred_element_type=jnp.float32)
    own_cols = lax.psum_scatter(
        partial_value.astype(jnp.bfloat16), ("tensor", "section"), scatter_dimension=1, tiled=True
    )
    owners = lax.axis_size("dp")
    slot_count = image_owner.shape[0] * image_owner.shape[1]
    img_rows = tok_rows // slot_count
    capacity = img_rows * max(1, slot_count // owners)
    live_len = jnp.where(
        jnp.arange(image_owner.shape[1])[None, :] < image_count[:, None], tile_count * TILE_TOK, 0
    ).reshape(slot_count)
    dest_owner = image_owner.reshape(slot_count)
    earlier = jnp.arange(slot_count)[None, :] < jnp.arange(slot_count)[:, None]
    same_owner = dest_owner[:, None] == dest_owner[None, :]
    offsets = jnp.sum(jnp.where(same_owner & earlier, live_len[None, :], 0), axis=1)
    tok_index = jnp.arange(img_rows)
    targets = dest_owner[:, None] * capacity + offsets[:, None] + tok_index[None, :]
    targets = jnp.where(tok_index[None, :] < live_len[:, None], targets, -1).reshape(tok_rows)
    placing = (jnp.arange(owners * capacity)[:, None] == targets[None, :]).astype(jnp.bfloat16)
    send_rows = jnp.dot(placing, own_cols, preferred_element_type=jnp.float32).astype(jnp.bfloat16)
    send_rows = send_rows.reshape(owners, capacity, col_block)
    norm_terms = jnp.einsum(
        "sik,kv->siv",
        lax.all_to_all(send_rows, "dp", split_axis=0, concat_axis=0, tiled=True),
        proj_weight,
        preferred_element_type=jnp.float32,
    )
    norm_terms = norm_terms.reshape(owners * capacity, norm_terms.shape[2])
    norm_grad = lax.psum_scatter(
        norm_terms.astype(jnp.bfloat16), ("tensor", "section"), scatter_dimension=0, tiled=True
    ).astype(jnp.float32)
    share_rows = norm_grad.shape[0]
    inputs = lax.dynamic_slice_in_dim(
        vision_states, group_index * share_rows, share_rows, 0
    ).astype(jnp.float32)
    centre = inputs - jnp.mean(inputs, axis=1, keepdims=True)
    inverse = lax.rsqrt(jnp.mean(centre * centre, axis=1, keepdims=True) + 1e-05)
    normed = centre * inverse
    scaled = norm_grad * norm_gain
    return (
        scaled
        - jnp.mean(scaled, axis=1, keepdims=True)
        - normed * jnp.mean(scaled * normed, axis=1, keepdims=True)
    ) * inverse


def solution(mesh):
    return jax.shard_map(
        per_device,
        mesh=mesh,
        in_specs=(
            P("dp", "section", None, "tensor"),
            P("section", None, "tensor", None),
            P("dp"),
            P("dp", None),
            P("dp", None),
            P(("tensor", "section"), None),
            P("dp", None),
            P(),
        ),
        out_specs=P(("dp", "tensor", "section"), None),
        check_vma=False,
    )
```

profile of v0, /device:TPU:0, one launch (start us, length us, event | category | flops | bytes accessed | tf_op | source)
XLA Modules:
  0.0 114.8 jit_solution(5340490339717253917)
XLA Ops:
  6.5 0.0 copy-start
  6.5 0.0 reduce-scatter.3.cloned.1.call-start
  6.5 0.0 copy-start.4
  6.5 0.0 copy-start.5
  6.5 0.0 copy-start.3
  6.6 6.2 %fusion = bf16[128,8192]{1,0:T(8,128)(2,1)} fusion(bf16[1,2,256,8192]{3,2,1,0:T(8,128)(2,1)} %param.9, bf16[128,2,256]{2,1,0:T(2,128)(2,1)} %bitcast.18), kind=kOutput, calls=%fused_computation.1 | convolution fusion | flops 1074790400 | bytes 10616832 | tf_op jit(solution)/shard_map/dot_general | solution.py:19
  12.8 0.0 copy-start.1
  12.8 0.0 reduce-scatter.3.cloned.1.call-update
  12.8 0.0 copy-done.4
  12.8 0.0 copy-done.5
  12.8 0.1 copy.13
  12.9 0.1 lt.55
  13.0 0.0 copy-done.3
  13.0 0.1 copy.14
  13.1 0.1 broadcast_in_dim_reshape.2
  13.2 0.2 select_reduce_fusion
  13.4 0.1 add_select_fusion
  13.4 0.1 select_n.25
  13.5 43.3 %reduce-scatter.3.cloned.1.call-done = bf16[128,1024]{1,0:T(8,128)(2,1)} async-done(((bf16[128,8192]{1,0:T(8,128)(2,1)}), bf16[128,1024]{1,0:T(8,128)(2,1)}) %reduce-scatter.3.cloned.1.call-update) | async-done | bytes 262160 | tf_op jit(solution)/shard_map/reduce_scatter | solution.py:20
  56.9 1.9 %convolution_convert_fusion = bf16[128,1024]{1,0:T(8,128)(2,1)} fusion(bf16[128,1024]{1,0:T(8,128)(2,1)} %reduce-scatter.3.cloned.1.call-done, s32[128]{0:T(128)S(1)} %select_n.25), kind=kOutput, calls=%fused_computation.6 | convolution fusion | flops 33701888 | bytes 524800 | tf_op jit(solution)/shard_map/dot_general | solution.py:38
  58.7 4.6 %all-to-all-start = ((bf16[4,32,1024]{2,1,0:T(8,128)(2,1)}), bf16[4,32,1024]{2,1,0:T(8,128)(2,1)S(1)}, u32[]{:S(2)}, u32[]{:S(2)}) async-start(bf16[4,32,1024]{2,1,0:T(8,128)(2,1)} %bitcast.3), calls=%async_computation.1 | async-start | bytes 524288 | tf_op jit(solution)/shard_map/all_to_all | solution.py:42
  63.3 0.0 copy-start.2
  63.3 0.0 reduce-scatter.5.cloned.1.call-start
  63.3 0.0 copy-done.1
  63.3 0.1 convert_reduce_fusion
  63.5 8.8 %all-to-all-done = bf16[4,32,1024]{2,1,0:T(8,128)(2,1)S(1)} async-done(((bf16[4,32,1024]{2,1,0:T(8,128)(2,1)}), bf16[4,32,1024]{2,1,0:T(8,128)(2,1)S(1)}, u32[]{:S(2)}, u32[]{:S(2)}) %all-to-all-start) | async-done | bytes 262176 | tf_op jit(solution)/shard_map/all_to_all | solution.py:42
  72.3 0.0 copy-done
  72.3 1.2 %fusion.4 = bf16[4,32,1280]{2,1,0:T(8,128)(2,1)} fusion(bf16[4,32,1024]{2,1,0:T(8,128)(2,1)S(1)} %all-to-all-done, bf16[1024,1280]{1,0:T(8,128)(2,1)S(1)} %copy-done), kind=kOutput, calls=%fused_computation.5 | convolution fusion | flops 335708160 | bytes 3211264 | tf_op jit(solution)/shard_map/sik,kv->siv/dot_general | solution.py:40
  73.5 0.0 reduce-scatter.5.cloned.1.call-update
  73.5 0.2 fusion.15
  73.7 31.8 %reduce-scatter.5.cloned.1.call-done = bf16[16,1280]{1,0:T(8,128)(2,1)} async-done(((bf16[128,1280]{1,0:T(8,128)(2,1)}), bf16[16,1280]{1,0:T(8,128)(2,1)}) %reduce-scatter.5.cloned.1.call-update) | async-done | bytes 40976 | tf_op jit(solution)/shard_map/reduce_scatter | solution.py:47
  105.5 0.0 copy-done.2
  105.5 1.0 fusion.16
  106.5 1.5 %fusion.14 = f32[16,1280]{1,0:T(8,128)} fusion(bf16[16,1280]{1,0:T(8,128)(2,1)} %reduce-scatter.5.cloned.1.call-done, f32[16]{0:T(128)S(1)} %get-tuple-element.7, f32[16]{0:T(128)S(1)} %add_rsqrt_fusion, f32[16]{0:T(128)S(1)} %broadcast_multiply_fusion.1, f32[16]{0:T(128)S(1)} %get-tuple-element.8, f32[1280]{0:T(1024)S(1)} %copy-done.2, ...), kind=kLoop, calls=%fused_computation.16 | loop fusion | flops 184320 | bytes 169220 | tf_op jit(solution)/shard_map/mul | solution.py:58
  (5 shorter events, 0.0 us)
Async XLA Ops:
  6.5 65.7 %copy-start = (bf16[1024,1280]{1,0:T(8,128)(2,1)S(1)}, bf16[1024,1280]{1,0:T(8,128)(2,1)}, u32[]{:S(2)}) copy-start(bf16[1024,1280]{1,0:T(8,128)(2,1)} %param.13) | copy-start | bytes 7864324
  6.5 50.3 %reduce-scatter.3.cloned.1.call-start = ((), (), s32[]{:S(2)}) async-start(), calls=%async_computation.3 | async-start | bytes 2359296 | tf_op jit(solution)/shard_map/reduce_scatter | solution.py:20
  6.5 6.3 %copy-start.4 = (s32[8,2]{0,1:T(2,128)S(1)}, s32[8,2]{0,1:T(2,128)}, u32[]{:S(2)}) copy-start(s32[8,2]{0,1:T(2,128)} %param.11) | copy-start | bytes 196
  6.5 6.3 %copy-start.5 = (s32[8]{0:T(128)S(1)}, s32[8]{0:T(128)}, u32[]{:S(2)}) copy-start(s32[8]{0:T(128)} %param.10) | copy-start | bytes 100
  6.5 6.5 %copy-start.3 = (s32[8,2]{0,1:T(2,128)S(1)}, s32[8,2]{0,1:T(2,128)}, u32[]{:S(2)}) copy-start(s32[8,2]{0,1:T(2,128)} %param.12) | copy-start | bytes 196
  12.8 50.6 %copy-start.1 = (bf16[128,1280]{1,0:T(8,128)(2,1)S(1)}, bf16[128,1280]{1,0:T(8,128)(2,1)}, u32[]{:S(2)}) copy-start(bf16[128,1280]{1,0:T(8,128)(2,1)} %param.14) | copy-start | bytes 983044
  58.7 13.5 %all-to-all-start = ((bf16[4,32,1024]{2,1,0:T(8,128)(2,1)}), bf16[4,32,1024]{2,1,0:T(8,128)(2,1)S(1)}, u32[]{:S(2)}, u32[]{:S(2)}) async-start(bf16[4,32,1024]{2,1,0:T(8,128)(2,1)} %bitcast.3), calls=%async_computation.1 | async-start | bytes 524288 | tf_op jit(solution)/shard_map/all_to_all | solution.py:42
  63.3 42.2 %copy-start.2 = (f32[1280]{0:T(1024)S(1)}, f32[1280]{0:T(1024)}, u32[]{:S(2)}) copy-start(f32[1280]{0:T(1024)} %param.15) | copy-start | bytes 15364
  63.3 42.2 %reduce-scatter.5.cloned.1.call-start = ((), (), s32[]{:S(2)}) async-start(), calls=%async_computation.4 | async-start | bytes 368640 | tf_op jit(solution)/shard_map/reduce_scatter | solution.py:47
Sparse Core Ops, SparseCore 0:
  12.9 43.8 reduce-scatter.2
  73.6 31.8 reduce-scatter.4
where the time goes:
time: 115 us
  waiting for transfers between devices  83.9 us (73%)
  between operations  13.5 us (12%)
  matrix products  9.31 us (8%)
  starting transfers between devices  4.61 us (4%)
  other arithmetic  3.09 us (3%)
    reduce_scatter x1, waiting for transfers between devices, per_device(): lax.psum_scatter(partial_value.astype(jnp.bfloat16), ('tensor', 'section'...  43.3 us
    reduce_scatter x1, waiting for transfers between devices, per_device(): lax.psum_scatter(norm_terms.astype(jnp.bfloat16), ('tensor', 'section'),...  31.8 us
    all_to_all x1, waiting for transfers between devices, per_device(): lax.all_to_all(send_rows, 'dp', split_axis=0, concat_axis=0, tiled=True)  8.78 us
    dot_general x1, matrix products, per_device(): jnp.dot(left_side, right_side, preferred_element_type=jnp.float32)  6.21 us
    all_to_all x1, starting transfers between devices, per_device(): lax.all_to_all(send_rows, 'dp', split_axis=0, concat_axis=0, tiled=True)  4.61 us
  transfers between devices with their start and end apart: 3, of which 3 were waited for; matrix products, arithmetic and copies ran while one was open for 1% of the time, Pallas kernels for 0%

commit v1 on v0

v1 whole, which is shorter than its diff:
```python
import functools
import jax
import jax.numpy as jnp
from jax import lax
from jax.experimental import pallas as pl
from jax.experimental.pallas import tpu as pltpu
from jax.sharding import PartitionSpec as P

TILE_TOK = 2
MESH = pl.DeviceIdType.MESH
F32 = jnp.float32
BF16 = jnp.bfloat16


def stage_of(q, bits):
    return bits - q.bit_length()


def block_mask(q, core, bits):
    mask = 0
    for step in range(bits):
        if q >> (bits - 1 - step) & 1:
            mask = mask + lax.shift_left(jnp.int32(1), jnp.int32((step + core) % bits))
    return mask


def xor(a, b, bits):
    total = 0
    for bit in range(bits):
        x, y = a // (1 << bit) % 2, b // (1 << bit) % 2
        total = total + (x + y - 2 * x * y) * (1 << bit)
    return total


def kernel(
    sizes, cnt_ref, til_ref, own_ref, grad_ref, w_hbm, proj_hbm, vis_hbm, gain_ref, out_ref,
    wbuf, pbuf, vbuf, sib_out, sib_in, local, half_out, half_in, term, pair_in, pair_out, chip_in,
    done, unit_in,
    w_sem, p_sem, v_sem, sib_s, sib_r, half_s, half_r, pair_s, pair_r, chip_s, chip_r, unit_s, unit_r,
):
    n_dp, n_t, bits, rows, cap, placed, share, unit, samples, slots = sizes
    groups = 2 * n_t
    dp, t, s = lax.axis_index("dp"), lax.axis_index("tensor"), lax.axis_index("section")
    g = t * 2 + s
    other = 1 - s
    col = wbuf.shape[2]
    units = share // unit
    early = placed <= rows

    def flip(t_index, step, core):
        bit = 1
        if bits > 1:
            shift = (step + core) % bits
            bit = sum(jnp.where(shift == i, 1 << i, 0) for i in range(bits))
        digit = t_index // bit % 2
        return t_index + (1 - 2 * digit) * bit

    def tensor_of(q, core):
        index = t
        for step in range(bits):
            if q >> (bits - 1 - step) & 1:
                index = flip(index, step, core)
        return index

    order = []
    for q in reversed(range(n_t)):
        order.append((q, True))
        if q < n_t - 1:
            order.append((q + 1, False))
    order.append((0, False))
    w_copies = {}
    for i, (q, sibling) in enumerate(order):
        core = other if sibling else s
        block = tensor_of(q, core) * 2 + core
        cp = pltpu.make_async_copy(
            w_hbm.at[:, pl.ds(pl.multiple_of(block * col, 128), col)], wbuf.at[i], w_sem.at[i]
        )
        cp.start()
        w_copies[q, sibling] = (i, cp)
    v_copy = pltpu.make_async_copy(vis_hbm.at[pl.ds(pl.multiple_of(g * share, 16), share)], vbuf, v_sem)
    v_copy.start()
    p_copy = pltpu.make_async_copy(proj_hbm, pbuf, p_sem)
    p_copy.start()

    dests, sources = [], []
    for k in range(units):
        row = g * share + k * unit
        to = row // cap
        at = dp * cap + row % cap
        dests.append((to, at // share, at % share // unit))
        src_dp = row // cap
        src_row = dp * cap + row % cap
        sources.append((src_dp, src_row // share))

    def is_me(d_index, g_index):
        return jnp.logical_and(d_index == dp, g_index == g)

    barrier = pltpu.get_barrier_semaphore()
    pl.semaphore_signal(barrier, inc=1, device_id=(dp, t, other), device_id_type=MESH)
    for m in range(1, n_t):
        pl.semaphore_signal(barrier, inc=1, device_id=(dp, xor(t, m, bits), s), device_id_type=MESH)
    expect = jnp.int32(n_t)
    for k in range(units):
        src_dp, src_g = sources[k]

        @pl.when(jnp.logical_not(is_me(src_dp, src_g)))
        def _():
            pl.semaphore_signal(barrier, inc=1, device_id=(src_dp, src_g // 2, src_g % 2), device_id_type=MESH)

        expect = expect + jnp.where(is_me(dests[k][0], dests[k][1]), 0, 1)

    img_rows = rows // slots
    per = slots // samples
    live, owner = [], []
    for j in range(slots):
        live.append(jnp.where(j % per < cnt_ref[j // per], til_ref[j // per, j % per] * TILE_TOK, 0))
        owner.append(own_ref[j // per, j % per])
    lane = lax.broadcasted_iota(jnp.int32, (1, rows), 1)
    slot, tok = lane // img_rows, lane % img_rows
    target = jnp.full((1, rows), -1, jnp.int32)
    for j in range(slots):
        base = owner[j] * cap
        for i in range(j):
            base = base + jnp.where(owner[i] == owner[j], live[i], 0)
        target = jnp.where(slot == j, jnp.where(tok < live[j], base + tok, -1), target)
    placing = (lax.broadcasted_iota(jnp.int32, (placed, rows), 0) == target).astype(F32).astype(BF16)

    left = jnp.concatenate([grad_ref[:, 0, :], grad_ref[:, 1, :]], axis=1)
    if early:
        left = jnp.dot(placing, left, preferred_element_type=F32).astype(BF16)

    def multiply(q, sibling):
        i, cp = w_copies[q, sibling]
        cp.wait()
        return jnp.dot(left, wbuf[i], preferred_element_type=F32)

    def sib_copy(q):
        return pltpu.make_async_remote_copy(
            sib_out.at[q], sib_in.at[q], sib_s.at[q], sib_r.at[q], device_id=(dp, t, other), device_id_type=MESH
        )

    def half_copy(q):
        to = flip(t, stage_of(q, bits), s)
        return pltpu.make_async_remote_copy(
            half_out.at[q], half_in.at[q], half_s.at[q], half_r.at[q], device_id=(dp, to, s), device_id_type=MESH
        )

    first = True
    for q, sibling in order:
        if sibling:
            sib_out[q] = multiply(q, True).astype(BF16)
            if first:
                pl.semaphore_wait(barrier, expect)
                first = False
            sib_copy(q).start()
        else:
            value = multiply(q, False)
            sib_copy(q).wait_recv()
            value = value + sib_in[q].astype(F32)
            if q > 0 and stage_of(q, bits) == 0:
                half_out[q] = value.astype(BF16)
                half_copy(q).start()
            else:
                local[q] = value

    v_copy.wait()
    states = vbuf[...].astype(F32)
    centre = states - jnp.mean(states, axis=1, keepdims=True)
    inverse = lax.rsqrt(jnp.mean(centre * centre, axis=1, keepdims=True) + 1e-05)
    normed = centre * inverse

    for q in reversed(range(n_t // 2)):
        value = local[q]
        for step in range(stage_of(q, bits)):
            sent = q + (n_t >> (step + 1))
            half_copy(sent).wait_recv()
            value = value + half_in[sent].astype(F32)
        if q > 0:
            half_out[q] = value.astype(BF16)
            half_copy(q).start()
    features = value.astype(BF16)
    if not early:
        features = jnp.dot(placing, features, preferred_element_type=F32).astype(BF16)
    p_copy.wait()
    product = jnp.dot(features, pbuf[...], preferred_element_type=F32).astype(BF16)
    for i in range(groups):
        term[i % 2, i // 2] = product[i * share:(i + 1) * share]

    pair = pltpu.make_async_remote_copy(
        term.at[other], pair_in, pair_s, pair_r, device_id=(dp, t, other), device_id_type=MESH
    )
    pair.start()
    pair.wait_recv()

    def chip_copy(m):
        return pltpu.make_async_remote_copy(
            pair_out.at[m], chip_in.at[m], chip_s.at[m], chip_r.at[m],
            device_id=(dp, xor(t, m, bits), s), device_id_type=MESH,
        )

    for m in range(1, n_t):
        to = xor(t, m, bits)
        pair_out[m] = (term[s, to].astype(F32) + pair_in[to].astype(F32)).astype(BF16)
        chip_copy(m).start()
    total = term[s, t].astype(F32) + pair_in[t].astype(F32)
    for m in range(1, n_t):
        chip_copy(m).wait_recv()
        total = total + chip_in[m].astype(F32)
    for k in range(units):
        done[k] = total[k * unit:(k + 1) * unit].astype(done.dtype)

    def unit_copy(k):
        to, to_g, at = dests[k]
        return pltpu.make_async_remote_copy(
            done.at[k], unit_in.at[at], unit_s.at[k], unit_r.at[at],
            device_id=(to, to_g // 2, to_g % 2), device_id_type=MESH,
        )

    for k in range(units):
        mine = is_me(dests[k][0], dests[k][1])

        @pl.when(mine)
        def _():
            unit_in[dests[k][2]] = done[k]

        @pl.when(jnp.logical_not(mine))
        def _():
            unit_copy(k).start()

    for k in range(units):

        @pl.when(jnp.logical_not(is_me(*sources[k])))
        def _():
            pltpu.make_async_remote_copy(
                done.at[k], unit_in.at[k], unit_s.at[k], unit_r.at[k],
                device_id=(sources[k][0], sources[k][1] // 2, sources[k][1] % 2), device_id_type=MESH,
            ).wait_recv()

    norm_grad = jnp.concatenate([unit_in[k] for k in range(units)], axis=0).astype(F32)
    scaled = norm_grad * gain_ref[...]
    out_ref[...] = (
        scaled
        - jnp.mean(scaled, axis=1, keepdims=True)
        - normed * jnp.mean(scaled * normed, axis=1, keepdims=True)
    ) * inverse

    for q in range(n_t):
        sib_copy(q).wait_send()
    for q in range(1, n_t):
        half_copy(q).wait_send()
    pair.wait_send()
    for m in range(1, n_t):
        chip_copy(m).wait_send()
    for k in range(units):

        @pl.when(jnp.logical_not(is_me(dests[k][0], dests[k][1])))
        def _():
            unit_copy(k).wait_send()


def solution(mesh):
    n_dp, n_t = mesh.shape["dp"], mesh.shape["tensor"]
    bits = n_t.bit_length() - 1

    def per_device(grad_kv, kv_weight, image_count, tile_count, image_owner, proj_weight, vision_states, norm_gain):
        rows, width = grad_kv.shape[0], proj_weight.shape[1]
        depth = 2 * grad_kv.shape[3]
        samples = image_owner.shape[0]
        slots = samples * image_owner.shape[1]
        cap = rows // slots * max(1, slots // n_dp)
        placed = n_dp * cap
        share = placed // (2 * n_t)
        unit = min(cap, share)
        units = share // unit
        dm = kv_weight.shape[3]
        col = dm // (2 * n_t)
        mid = rows
        sizes = (n_dp, n_t, bits, rows, cap, placed, share, unit, samples, slots)
        moved = BF16 if unit % 16 == 0 else F32
        vmem, smem, hbm = (pl.BlockSpec(memory_space=m) for m in (pltpu.VMEM, pltpu.SMEM, pl.ANY))
        dma = pltpu.SemaphoreType.DMA
        return pl.pallas_call(
            functools.partial(kernel, sizes),
            out_shape=jax.ShapeDtypeStruct((share, width), F32),
            in_specs=[smem, smem, smem, vmem, hbm, hbm, hbm, vmem],
            out_specs=vmem,
            scratch_shapes=[
                pltpu.VMEM((2 * n_t, depth, col), BF16),
                pltpu.VMEM((col, width), BF16),
                pltpu.VMEM((share, width), BF16),
                pltpu.VMEM((n_t, mid, col), BF16),
                pltpu.VMEM((n_t, mid, col), BF16),
                pltpu.VMEM((max(1, n_t // 2), mid, col), F32),
                pltpu.VMEM((n_t, mid, col), BF16),
                pltpu.VMEM((n_t, mid, col), BF16),
                pltpu.VMEM((2, n_t, share, width), BF16),
                pltpu.VMEM((n_t, share, width), BF16),
                pltpu.VMEM((n_t, share, width), BF16),
                pltpu.VMEM((n_t, share, width), BF16),
                pltpu.VMEM((units, unit, width), moved),
                pltpu.VMEM((units, unit, width), moved),
                dma((2 * n_t,)), dma, dma,
                dma((n_t,)), dma((n_t,)), dma((n_t,)), dma((n_t,)), dma, dma,
                dma((n_t,)), dma((n_t,)), dma((units,)), dma((units,)),
            ],
            compiler_params=pltpu.CompilerParams(
                collective_id=0, has_side_effects=True, vmem_limit_bytes=40 * 1024 * 1024
            ),
        )(
            image_count, tile_count, image_owner, grad_kv.reshape(rows, 2, grad_kv.shape[3]),
            kv_weight.reshape(depth, dm), proj_weight, vision_states, norm_gain.reshape(1, width),
        )

    return jax.shard_map(
        per_device,
        mesh=mesh,
        in_specs=(
            P("dp", "section", None, "tensor"),
            P("section", None, "tensor", None),
            P("dp"),
            P("dp", None),
            P("dp", None),
            P(("tensor", "section"), None),
            P("dp", None),
            P(),
        ),
        out_specs=P(("dp", "tensor", "section"), None),
        check_vma=False,
    )
```

time: 115 us -> 39.3 us (0.34)
  the two profiles are of different devices: /device:TPU:0 before, /device:TPU:6 now
where the time goes in v1:
time: 39.3 us; the launch traced here: 38.9 us
  Pallas kernels  28.4 us (72%)
  local copies, waits for them, and re-layouts  10.5 us (27%)
    pallas_call x1, Pallas kernels, per_device(): pl.pallas_call(functools.partial(kernel, sizes), out_shape=jax.ShapeDtype...  28.4 us
    unnamed x13, local copies, waits for them, and re-layouts  9.79 us

profile of v1, /device:TPU:6, one launch (start us, length us, event | category | flops | bytes accessed | tf_op | source)
XLA Modules:
  0.0 38.9 jit_solution(11250680429341878106)
XLA Ops:
  0.0 0.8 %copy.9.til_ref = s32[8,2]{1,0:T(8,128)S(1)} copy(s32[8,2]{0,1:T(2,128)} %param.11) | data formatting | bytes 128 | tf_op args[3]
  0.8 0.8 %copy.10.own_ref = s32[8,2]{1,0:T(8,128)S(1)} copy(s32[8,2]{0,1:T(2,128)} %param.12) | data formatting | bytes 128 | tf_op args[4]
  1.5 0.7 %reshape.11.gain_ref = f32[1,1280]{1,0:T(1,128)S(1)} reshape(f32[1280]{0:T(1024)} %param.15) | data formatting | bytes 10240 | tf_op jit(solution)/shard_map/reshape | solution.py:311
  2.2 0.0 copy-start
  2.2 3.4 %copy-done = bf16[1,2,256,8192]{3,2,1,0:T(8,128)(2,1)S(1)} copy-done((bf16[1,2,256,8192]{3,2,1,0:T(8,128)(2,1)S(1)}, bf16[1,2,256,8192]{3,2,1,0:T(8,128)(2,1)}, u32[]{:S(2)}) %copy-start) | copy-done | bytes 8388632
  5.6 0.0 copy-start.1
  5.6 1.7 %copy-done.1 = bf16[1024,1280]{1,0:T(8,128)(2,1)S(1)} copy-done((bf16[1024,1280]{1,0:T(8,128)(2,1)S(1)}, bf16[1024,1280]{1,0:T(8,128)(2,1)}, u32[]{:S(2)}) %copy-start.1) | copy-done | bytes 2621464
  7.3 0.0 copy-start.2
  7.3 1.0 %copy-done.2 = bf16[128,1280]{1,0:T(8,128)(2,1)S(1)} copy-done((bf16[128,1280]{1,0:T(8,128)(2,1)S(1)}, bf16[128,1280]{1,0:T(8,128)(2,1)}, u32[]{:S(2)}) %copy-start.2) | copy-done | bytes 327704
  8.3 0.0 copy-start.3
  8.3 0.9 %copy-done.3 = bf16[128,1,2,256]{3,2,1,0:T(2,128)(2,1)S(1)} copy-done((bf16[128,1,2,256]{3,2,1,0:T(2,128)(2,1)S(1)}, bf16[128,1,2,256]{3,2,1,0:T(2,128)(2,1)}, u32[]{:S(2)}) %copy-start.3) | copy-done | bytes 131096
  9.2 0.0 copy-start.4
  9.2 0.7 %copy-done.4 = s32[8]{0:T(128)S(1)} copy-done((s32[8]{0:T(128)S(1)}, s32[8]{0:T(128)}, u32[]{:S(2)}) %copy-start.4) | copy-done | bytes 56
  9.9 28.4 %shard_map.82 = f32[16,1280]{1,0:T(8,128)S(1)} custom-call(s32[8]{0:T(128)S(1)} %copy-done.4, s32[8,2]{1,0:T(8,128)S(1)} %copy.9.til_ref, s32[8,2]{1,0:T(8,128)S(1)} %copy.10.own_ref, bf16[128,2,256]{2,1,0:T(2,128)(2,1)S(1)} %bitcast.3, bf16[512,8192]{1,0:T(8,128)(2,1)S(1)} %bitcast.2, bf16[1024,1280]{1,0:T(8,128)(2,1)S(1)} %copy-done.1, ...), custom_call_target="tpu_custom_call" | custom-call | tf_op jit(solution)/shard_map/pallas_call | solution.py:282
  38.3 0.6 %copy.12 = f32[16,1280]{1,0:T(8,128)} copy(f32[16,1280]{1,0:T(8,128)S(1)} %shard_map.82) | data formatting | bytes 163840
Async XLA Ops:
  2.2 3.4 %copy-start = (bf16[1,2,256,8192]{3,2,1,0:T(8,128)(2,1)S(1)}, bf16[1,2,256,8192]{3,2,1,0:T(8,128)(2,1)}, u32[]{:S(2)}) copy-start(bf16[1,2,256,8192]{3,2,1,0:T(8,128)(2,1)} %param.9) | copy-start | bytes 25165828
  5.6 1.7 %copy-start.1 = (bf16[1024,1280]{1,0:T(8,128)(2,1)S(1)}, bf16[1024,1280]{1,0:T(8,128)(2,1)}, u32[]{:S(2)}) copy-start(bf16[1024,1280]{1,0:T(8,128)(2,1)} %proj_hbm.1) | copy-start | bytes 7864324
  7.3 1.0 %copy-start.2 = (bf16[128,1280]{1,0:T(8,128)(2,1)S(1)}, bf16[128,1280]{1,0:T(8,128)(2,1)}, u32[]{:S(2)}) copy-start(bf16[128,1280]{1,0:T(8,128)(2,1)} %vis_hbm.1) | copy-start | bytes 983044
  8.3 0.9 %copy-start.3 = (bf16[128,1,2,256]{3,2,1,0:T(2,128)(2,1)S(1)}, bf16[128,1,2,256]{3,2,1,0:T(2,128)(2,1)}, u32[]{:S(2)}) copy-start(bf16[128,1,2,256]{3,2,1,0:T(2,128)(2,1)} %param.8) | copy-start | bytes 393220
  9.2 0.7 %copy-start.4 = (s32[8]{0:T(128)S(1)}, s32[8]{0:T(128)}, u32[]{:S(2)}) copy-start(s32[8]{0:T(128)} %cnt_ref.1) | copy-start | bytes 100

commit v2 on v1

--- a/solution.py
+++ b/solution.py
@@ -33,10 +33,10 @@
 
 
 def kernel(
-    sizes, cnt_ref, til_ref, own_ref, grad_ref, w_hbm, proj_hbm, vis_hbm, gain_ref, out_ref,
-    wbuf, pbuf, vbuf, sib_out, sib_in, local, half_out, half_in, term, pair_in, pair_out, chip_in,
+    sizes, cnt_ref, til_ref, own_ref, grad_hbm, w_hbm, proj_hbm, vis_hbm, gain_hbm, out_ref,
+    grad_ref, gain_ref,    wbuf, pbuf, vbuf, sib_out, sib_in, local, half_out, half_in, term, pair_in, pair_out, chip_in,
     done, unit_in,
-    w_sem, p_sem, v_sem, sib_s, sib_r, half_s, half_r, pair_s, pair_r, chip_s, chip_r, unit_s, unit_r,
+    g_sem, n_sem, w_sem, p_sem, v_sem, sib_s, sib_r, half_s, half_r, pair_s, pair_r, chip_s, chip_r, unit_s, unit_r,
 ):
     n_dp, n_t, bits, rows, cap, placed, share, unit, samples, slots = sizes
     groups = 2 * n_t
@@ -68,6 +68,8 @@
         if q < n_t - 1:
             order.append((q + 1, False))
     order.append((0, False))
+    g_copy = pltpu.make_async_copy(grad_hbm, grad_ref, g_sem)
+    g_copy.start()
     w_copies = {}
     for i, (q, sibling) in enumerate(order):
         core = other if sibling else s
@@ -81,6 +83,8 @@
     v_copy.start()
     p_copy = pltpu.make_async_copy(proj_hbm, pbuf, p_sem)
     p_copy.start()
+    n_copy = pltpu.make_async_copy(gain_hbm, gain_ref, n_sem)
+    n_copy.start()
 
     dests, sources = [], []
     for k in range(units):
@@ -113,8 +117,8 @@
     per = slots // samples
     live, owner = [], []
     for j in range(slots):
-        live.append(jnp.where(j % per < cnt_ref[j // per], til_ref[j // per, j % per] * TILE_TOK, 0))
-        owner.append(own_ref[j // per, j % per])
+        live.append(jnp.where(j % per < cnt_ref[j // per], til_ref[j % per, j // per] * TILE_TOK, 0))
+        owner.append(own_ref[j % per, j // per])
     lane = lax.broadcasted_iota(jnp.int32, (1, rows), 1)
     slot, tok = lane // img_rows, lane % img_rows
     target = jnp.full((1, rows), -1, jnp.int32)
@@ -125,6 +129,7 @@
         target = jnp.where(slot == j, jnp.where(tok < live[j], base + tok, -1), target)
     placing = (lax.broadcasted_iota(jnp.int32, (placed, rows), 0) == target).astype(F32).astype(BF16)
 
+    g_copy.wait()
     left = jnp.concatenate([grad_ref[:, 0, :], grad_ref[:, 1, :]], axis=1)
     if early:
         left = jnp.dot(placing, left, preferred_element_type=F32).astype(BF16)
@@ -164,6 +169,8 @@
                 local[q] = value
 
     v_copy.wait()
+    n_copy.wait()
+    gain = gain_ref[...].reshape(1, gain_ref.shape[0])
     states = vbuf[...].astype(F32)
     centre = states - jnp.mean(states, axis=1, keepdims=True)
     inverse = lax.rsqrt(jnp.mean(centre * centre, axis=1, keepdims=True) + 1e-05)
@@ -237,7 +244,7 @@
             ).wait_recv()
 
     norm_grad = jnp.concatenate([unit_in[k] for k in range(units)], axis=0).astype(F32)
-    scaled = norm_grad * gain_ref[...]
+    scaled = norm_grad * gain
     out_ref[...] = (
         scaled
         - jnp.mean(scaled, axis=1, keepdims=True)
@@ -277,14 +284,16 @@
         mid = rows
         sizes = (n_dp, n_t, bits, rows, cap, placed, share, unit, samples, slots)
         moved = BF16 if unit % 16 == 0 else F32
-        vmem, smem, hbm = (pl.BlockSpec(memory_space=m) for m in (pltpu.VMEM, pltpu.SMEM, pl.ANY))
+        vmem, smem, hbm = (pl.BlockSpec(memory_space=m) for m in (pltpu.VMEM, pltpu.SMEM, pltpu.HBM))
         dma = pltpu.SemaphoreType.DMA
         return pl.pallas_call(
             functools.partial(kernel, sizes),
             out_shape=jax.ShapeDtypeStruct((share, width), F32),
-            in_specs=[smem, smem, smem, vmem, hbm, hbm, hbm, vmem],
+            in_specs=[smem, smem, smem, hbm, hbm, hbm, hbm, hbm],
             out_specs=vmem,
             scratch_shapes=[
+                pltpu.VMEM((rows, 2, grad_kv.shape[3]), BF16),
+                pltpu.VMEM((width,), F32),
                 pltpu.VMEM((2 * n_t, depth, col), BF16),
                 pltpu.VMEM((col, width), BF16),
                 pltpu.VMEM((share, width), BF16),
@@ -299,16 +308,16 @@
                 pltpu.VMEM((n_t, share, width), BF16),
                 pltpu.VMEM((units, unit, width), moved),
                 pltpu.VMEM((units, unit, width), moved),
-                dma((2 * n_t,)), dma, dma,
+                dma, dma, dma((2 * n_t,)), dma, dma,
                 dma((n_t,)), dma((n_t,)), dma((n_t,)), dma((n_t,)), dma, dma,
                 dma((n_t,)), dma((n_t,)), dma((units,)), dma((units,)),
             ],
             compiler_params=pltpu.CompilerParams(
-                collective_id=0, has_side_effects=True, vmem_limit_bytes=40 * 1024 * 1024
+                collective_id=0, has_side_effects=True, vmem_limit_bytes=56 * 1024 * 1024
             ),
         )(
-            image_count, tile_count, image_owner, grad_kv.reshape(rows, 2, grad_kv.shape[3]),
-            kv_weight.reshape(depth, dm), proj_weight, vision_states, norm_gain.reshape(1, width),
+            image_count, tile_count.T, image_owner.T, grad_kv.reshape(rows, 2, grad_kv.shape[3]),
+            kv_weight.reshape(depth, dm), proj_weight, vision_states, norm_gain,
         )
 
     return jax.shard_map(

time: 39.3 us -> 31.4 us (0.80)
  local copies, waits for them, and re-layouts: 10.5 us -> 1.53 us
  Pallas kernels: 28.4 us -> 29.7 us
    unnamed x13 -> x1, local copies, waits for them, and re-layouts: 9.79 us -> 1.53 us
    pallas_call x1, Pallas kernels: 28.4 us -> 29.7 us  [per_device(): pl.pallas_call(functools.partial(kernel, sizes), out_shape=jax.ShapeDtype...]
    reshape x1 -> x0, local copies, waits for them, and re-layouts: 0.7 us -> none  [per_device(): norm_gain.reshape(1, width)]
where the time goes in v2:
time: 31.4 us; the launch traced here: 31.3 us
  Pallas kernels  29.7 us (95%)
  local copies, waits for them, and re-layouts  1.53 us (5%)
    pallas_call x1, Pallas kernels, per_device(): pl.pallas_call(functools.partial(kernel, sizes), out_shape=jax.ShapeDtype...  29.7 us
    unnamed x1, local copies, waits for them, and re-layouts  1.53 us

profile of v2, /device:TPU:6, one launch (start us, length us, event | category | flops | bytes accessed | tf_op | source)
XLA Modules:
  0.0 31.3 jit_solution(16224422537866443191)
XLA Ops:
  0.0 29.7 %shard_map.82 = f32[16,1280]{1,0:T(8,128)} custom-call(s32[8]{0:T(128)} %cnt_ref.1, s32[2,8]{1,0:T(2,128)} %bitcast.6, s32[2,8]{1,0:T(2,128)} %bitcast.7, bf16[128,2,256]{2,1,0:T(2,128)(2,1)} %bitcast.5, bf16[512,8192]{1,0:T(8,128)(2,1)} %bitcast.4, bf16[1024,1280]{1,0:T(8,128)(2,1)} %proj_hbm.1, bf16[128,1280]{1,0:T(8,128)(2,1)} %vis_hbm.1, f32[1280]{0:T(1024)} %gain_hbm.1), custom_call_target="tpu_custom_call" | custom-call | tf_op jit(solution)/shard_map/pallas_call | solution.py:289
  29.7 1.5 %copy.10 = f32[16,1280]{1,0:T(8,128)} copy(f32[16,1280]{1,0:T(8,128)} %shard_map.82) | data formatting | bytes 163840

commit v3 on v2

v3 whole, which is shorter than its diff:
```python
import functools
import jax
import jax.numpy as jnp
from jax import lax
from jax.experimental import pallas as pl
from jax.experimental.pallas import tpu as pltpu
from jax.sharding import PartitionSpec as P

TILE_TOK = 2
PIECES = 2
BANDS = 2
MESH = pl.DeviceIdType.MESH
F32 = jnp.float32
BF16 = jnp.bfloat16


def stage_of(q, bits):
    return bits - q.bit_length()


def block_mask(q, core, bits):
    mask = 0
    for step in range(bits):
        if q >> (bits - 1 - step) & 1:
            mask = mask + lax.shift_left(jnp.int32(1), jnp.int32((step + core) % bits))
    return mask


def xor(a, b, bits):
    total = 0
    for bit in range(bits):
        x, y = a // (1 << bit) % 2, b // (1 << bit) % 2
        total = total + (x + y - 2 * x * y) * (1 << bit)
    return total


def kernel(
    sizes, cnt_ref, til_ref, own_ref, grad_hbm, w_hbm, proj_hbm, vis_hbm, gain_hbm, out_ref,
    grad_ref, gain_ref,    wbuf, pbuf, vbuf, sib_out, sib_in, local, half_out, half_in, term, pair_in, pair_out, chip_in,
    done, unit_in,
    g_sem, n_sem, w_sem, p_sem, v_sem, sib_s, sib_r, half_s, half_r, pair_s, pair_r, chip_s, chip_r, unit_s, unit_r,
):
    n_dp, n_t, bits, rows, cap, placed, share, unit, samples, slots = sizes
    groups = 2 * n_t
    dp, t, s = lax.axis_index("dp"), lax.axis_index("tensor"), lax.axis_index("section")
    g = t * 2 + s
    other = 1 - s
    piece = wbuf.shape[2]
    wide = term.shape[4]
    units = share // unit
    early = placed <= rows

    def flip(t_index, step, core):
        bit = 1
        if bits > 1:
            shift = (step + core) % bits
            bit = sum(jnp.where(shift == i, 1 << i, 0) for i in range(bits))
        digit = t_index // bit % 2
        return t_index + (1 - 2 * digit) * bit

    def tensor_of(q, core):
        index = t
        for step in range(bits):
            if q >> (bits - 1 - step) & 1:
                index = flip(index, step, core)
        return index

    pieces = [(q, c) for q in reversed(range(n_t)) for c in range(PIECES)]
    order = [(pieces[0], True)]
    for i, here in enumerate(pieces[1:]):
        order += [(here, True), (pieces[i], False)]
    order += [(pieces[-1], False)]
    g_copy = pltpu.make_async_copy(grad_hbm, grad_ref, g_sem)
    g_copy.start()
    w_copies = {}
    for i, ((q, c), sibling) in enumerate(order):
        core = other if sibling else s
        block = tensor_of(q, core) * 2 + core
        cp = pltpu.make_async_copy(
            w_hbm.at[:, pl.ds(pl.multiple_of((block * PIECES + c) * piece, 128), piece)], wbuf.at[i], w_sem.at[i]
        )
        cp.start()
        w_copies[(q, c), sibling] = (i, cp)
    v_copy = pltpu.make_async_copy(vis_hbm.at[pl.ds(pl.multiple_of(g * share, 16), share)], vbuf, v_sem)
    v_copy.start()
    p_copy = pltpu.make_async_copy(proj_hbm, pbuf, p_sem)
    p_copy.start()
    n_copy = pltpu.make_async_copy(gain_hbm, gain_ref, n_sem)
    n_copy.start()

    dests, sources = [], []
    for k in range(units):
        row = g * share + k * unit
        to = row // cap
        at = dp * cap + row % cap
        dests.append((to, at // share, at % share // unit))
        src_dp = row // cap
        src_row = dp * cap + row % cap
        sources.append((src_dp, src_row // share))

    def is_me(d_index, g_index):
        return jnp.logical_and(d_index == dp, g_index == g)

    barrier = pltpu.get_barrier_semaphore()
    pl.semaphore_signal(barrier, inc=1, device_id=(dp, t, other), device_id_type=MESH)
    for m in range(1, n_t):
        pl.semaphore_signal(barrier, inc=1, device_id=(dp, xor(t, m, bits), s), device_id_type=MESH)
    expect = jnp.int32(n_t)
    for k in range(units):
        src_dp, src_g = sources[k]

        @pl.when(jnp.logical_not(is_me(src_dp, src_g)))
        def _():
            pl.semaphore_signal(barrier, inc=1, device_id=(src_dp, src_g // 2, src_g % 2), device_id_type=MESH)

        expect = expect + jnp.where(is_me(dests[k][0], dests[k][1]), 0, 1)

    img_rows = rows // slots
    per = slots // samples
    live, owner = [], []
    for j in range(slots):
        live.append(jnp.where(j % per < cnt_ref[j // per], til_ref[j % per, j // per] * TILE_TOK, 0))
        owner.append(own_ref[j % per, j // per])
    lane = lax.broadcasted_iota(jnp.int32, (1, rows), 1)
    slot, tok = lane // img_rows, lane % img_rows
    target = jnp.full((1, rows), -1, jnp.int32)
    for j in range(slots):
        base = owner[j] * cap
        for i in range(j):
            base = base + jnp.where(owner[i] == owner[j], live[i], 0)
        target = jnp.where(slot == j, jnp.where(tok < live[j], base + tok, -1), target)
    placing = (lax.broadcasted_iota(jnp.int32, (placed, rows), 0) == target).astype(F32).astype(BF16)

    g_copy.wait()
    left = jnp.concatenate([grad_ref[:, 0, :], grad_ref[:, 1, :]], axis=1)
    if early:
        left = jnp.dot(placing, left, preferred_element_type=F32).astype(BF16)

    def multiply(here, sibling):
        i, cp = w_copies[here, sibling]
        cp.wait()
        return jnp.dot(left, wbuf[i], preferred_element_type=F32)

    def sib_copy(here):
        at = here[0] * PIECES + here[1]
        return pltpu.make_async_remote_copy(
            sib_out.at[at], sib_in.at[at], sib_s.at[at], sib_r.at[at], device_id=(dp, t, other), device_id_type=MESH
        )

    def half_copy(here):
        at = here[0] * PIECES + here[1]
        to = flip(t, stage_of(here[0], bits), s)
        return pltpu.make_async_remote_copy(
            half_out.at[at], half_in.at[at], half_s.at[at], half_r.at[at], device_id=(dp, to, s), device_id_type=MESH
        )

    def gathered(here, value):
        q, c = here
        for step in range(stage_of(q, bits)):
            sent = q + (n_t >> (step + 1))
            half_copy((sent, c)).wait_recv()
            value = value + half_in[sent * PIECES + c].astype(F32)
        return value

    def send_half(here, value):
        half_out[here[0] * PIECES + here[1]] = value.astype(BF16)
        half_copy(here).start()

    waiting = []
    for count, (here, sibling) in enumerate(order):
        q, c = here
        if sibling:
            sib_out[q * PIECES + c] = multiply(here, True).astype(BF16)
            if count == 0:
                pl.semaphore_wait(barrier, expect)
            sib_copy(here).start()
            continue
        if q == 0 and c == PIECES - 2:
            for q_held, c_held in waiting:
                send_half((q_held, c_held), gathered((q_held, c_held), local[q_held * PIECES + c_held]))
            waiting = []
        value = multiply(here, False)
        sib_copy(here).wait_recv()
        value = value + sib_in[q * PIECES + c].astype(F32)
        if q > 0 and stage_of(q, bits) == 0:
            send_half(here, value)
        else:
            local[q * PIECES + c] = value
            if q > 0:
                waiting.append(here)

    v_copy.wait()
    n_copy.wait()
    gain = gain_ref[...].reshape(1, gain_ref.shape[0])
    states = vbuf[...].astype(F32)
    centre = states - jnp.mean(states, axis=1, keepdims=True)
    inverse = lax.rsqrt(jnp.mean(centre * centre, axis=1, keepdims=True) + 1e-05)
    normed = centre * inverse

    features = jnp.concatenate(
        [gathered((0, c), local[c]).astype(BF16) for c in range(PIECES)], axis=1
    )
    if not early:
        features = jnp.dot(placing, features, preferred_element_type=F32).astype(BF16)
    p_copy.wait()

    def pair_copy(b):
        return pltpu.make_async_remote_copy(
            term.at[b, other], pair_in.at[b], pair_s.at[b], pair_r.at[b],
            device_id=(dp, t, other), device_id_type=MESH,
        )

    def chip_copy(b, m):
        at = b * n_t + m
        return pltpu.make_async_remote_copy(
            pair_out.at[at], chip_in.at[at], chip_s.at[at], chip_r.at[at],
            device_id=(dp, xor(t, m, bits), s), device_id_type=MESH,
        )

    def unit_copy(b, k):
        to, to_g, at = dests[k]
        return pltpu.make_async_remote_copy(
            done.at[b * units + k], unit_in.at[b * units + at], unit_s.at[b * units + k], unit_r.at[b * units + at],
            device_id=(to, to_g // 2, to_g % 2), device_id_type=MESH,
        )

    for b in range(BANDS):
        product = jnp.dot(features, pbuf[:, b * wide:(b + 1) * wide], preferred_element_type=F32).astype(BF16)
        for i in range(groups):
            term[b, i % 2, i // 2] = product[i * share:(i + 1) * share]
        pair_copy(b).start()
    for b in range(BANDS):
        pair_copy(b).wait_recv()
        for m in range(1, n_t):
            to = xor(t, m, bits)
            pair_out[b * n_t + m] = (term[b, s, to].astype(F32) + pair_in[b, to].astype(F32)).astype(BF16)
            chip_copy(b, m).start()
    for b in range(BANDS):
        total = term[b, s, t].astype(F32) + pair_in[b, t].astype(F32)
        for m in range(1, n_t):
            chip_copy(b, m).wait_recv()
            total = total + chip_in[b * n_t + m].astype(F32)
        for k in range(units):
            done[b * units + k] = total[k * unit:(k + 1) * unit].astype(done.dtype)
            mine = is_me(dests[k][0], dests[k][1])

            @pl.when(mine)
            def _():
                unit_in[b * units + dests[k][2]] = done[b * units + k]

            @pl.when(jnp.logical_not(mine))
            def _():
                unit_copy(b, k).start()

    for b in range(BANDS):
        for k in range(units):

            @pl.when(jnp.logical_not(is_me(*sources[k])))
            def _():
                at = b * units + k
                pltpu.make_async_remote_copy(
                    done.at[at], unit_in.at[at], unit_s.at[at], unit_r.at[at],
                    device_id=(sources[k][0], sources[k][1] // 2, sources[k][1] % 2), device_id_type=MESH,
                ).wait_recv()

    norm_grad = jnp.concatenate(
        [jnp.concatenate([unit_in[b * units + k] for k in range(units)], axis=0) for b in range(BANDS)], axis=1
    ).astype(F32)
    scaled = norm_grad * gain
    out_ref[...] = (
        scaled
        - jnp.mean(scaled, axis=1, keepdims=True)
        - normed * jnp.mean(scaled * normed, axis=1, keepdims=True)
    ) * inverse

    for here in pieces:
        sib_copy(here).wait_send()
        if here[0] > 0:
            half_copy(here).wait_send()
    for b in range(BANDS):
        pair_copy(b).wait_send()
        for m in range(1, n_t):
            chip_copy(b, m).wait_send()
        for k in range(units):

            @pl.when(jnp.logical_not(is_me(dests[k][0], dests[k][1])))
            def _():
                unit_copy(b, k).wait_send()


def solution(mesh):
    n_dp, n_t = mesh.shape["dp"], mesh.shape["tensor"]
    bits = n_t.bit_length() - 1

    def per_device(grad_kv, kv_weight, image_count, tile_count, image_owner, proj_weight, vision_states, norm_gain):
        rows, width = grad_kv.shape[0], proj_weight.shape[1]
        depth = 2 * grad_kv.shape[3]
        samples = image_owner.shape[0]
        slots = samples * image_owner.shape[1]
        cap = rows // slots * max(1, slots // n_dp)
        placed = n_dp * cap
        share = placed // (2 * n_t)
        unit = min(cap, share)
        units = share // unit
        dm = kv_weight.shape[3]
        col = dm // (2 * n_t)
        piece = col // PIECES
        wide = width // BANDS
        sizes = (n_dp, n_t, bits, rows, cap, placed, share, unit, samples, slots)
        moved = BF16 if unit % 16 == 0 else F32
        vmem, smem, hbm = (pl.BlockSpec(memory_space=m) for m in (pltpu.VMEM, pltpu.SMEM, pltpu.HBM))
        dma = pltpu.SemaphoreType.DMA
        return pl.pallas_call(
            functools.partial(kernel, sizes),
            out_shape=jax.ShapeDtypeStruct((share, width), F32),
            in_specs=[smem, smem, smem, hbm, hbm, hbm, hbm, hbm],
            out_specs=vmem,
            scratch_shapes=[
                pltpu.VMEM((rows, 2, grad_kv.shape[3]), BF16),
                pltpu.VMEM((width,), F32),
                pltpu.VMEM((2 * n_t * PIECES, depth, piece), BF16),
                pltpu.VMEM((col, width), BF16),
                pltpu.VMEM((share, width), BF16),
                pltpu.VMEM((n_t * PIECES, rows, piece), BF16),
                pltpu.VMEM((n_t * PIECES, rows, piece), BF16),
                pltpu.VMEM((n_t * PIECES // 2, rows, piece), F32),
                pltpu.VMEM((n_t * PIECES, rows, piece), BF16),
                pltpu.VMEM((n_t * PIECES, rows, piece), BF16),
                pltpu.VMEM((BANDS, 2, n_t, share, wide), BF16),
                pltpu.VMEM((BANDS, n_t, share, wide), BF16),
                pltpu.VMEM((BANDS * n_t, share, wide), BF16),
                pltpu.VMEM((BANDS * n_t, share, wide), BF16),
                pltpu.VMEM((BANDS * units, unit, wide), moved),
                pltpu.VMEM((BANDS * units, unit, wide), moved),
                dma, dma, dma((2 * n_t * PIECES,)), dma, dma,
                dma((n_t * PIECES,)), dma((n_t * PIECES,)), dma((n_t * PIECES,)), dma((n_t * PIECES,)),
                dma((BANDS,)), dma((BANDS,)), dma((BANDS * n_t,)), dma((BANDS * n_t,)),
                dma((BANDS * units,)), dma((BANDS * units,)),
            ],
            compiler_params=pltpu.CompilerParams(
                collective_id=0, has_side_effects=True, vmem_limit_bytes=56 * 1024 * 1024
            ),
        )(
            image_count, tile_count.T, image_owner.T, grad_kv.reshape(rows, 2, grad_kv.shape[3]),
            kv_weight.reshape(depth, dm), proj_weight, vision_states, norm_gain,
        )

    return jax.shard_map(
        per_device,
        mesh=mesh,
        in_specs=(
            P("dp", "section", None, "tensor"),
            P("section", None, "tensor", None),
            P("dp"),
            P("dp", None),
            P("dp", None),
            P(("tensor", "section"), None),
            P("dp", None),
            P(),
        ),
        out_specs=P(("dp", "tensor", "section"), None),
        check_vma=False,
    )
```

time: 31.4 us -> 31.4 us (level)
  no operation moved by 1% of the time
where the time goes in v3:
time: 31.4 us; the launch traced here: 31.3 us
  Pallas kernels  29.7 us (95%)
  local copies, waits for them, and re-layouts  1.53 us (5%)
    pallas_call x1, Pallas kernels, per_device(): pl.pallas_call(functools.partial(kernel, sizes), out_shape=jax.ShapeDtype...  29.7 us
    unnamed x1, local copies, waits for them, and re-layouts  1.53 us

profile of v3, /device:TPU:6, one launch (start us, length us, event | category | flops | bytes accessed | tf_op | source)
XLA Modules:
  0.0 31.3 jit_solution(14834687377000307083)
XLA Ops:
  0.0 29.7 %shard_map.82 = f32[16,1280]{1,0:T(8,128)} custom-call(s32[8]{0:T(128)} %cnt_ref.1, s32[2,8]{1,0:T(2,128)} %bitcast.6, s32[2,8]{1,0:T(2,128)} %bitcast.7, bf16[128,2,256]{2,1,0:T(2,128)(2,1)} %bitcast.5, bf16[512,8192]{1,0:T(8,128)(2,1)} %bitcast.4, bf16[1024,1280]{1,0:T(8,128)(2,1)} %proj_hbm.1, bf16[128,1280]{1,0:T(8,128)(2,1)} %vis_hbm.1, f32[1280]{0:T(1024)} %gain_hbm.1), custom_call_target="tpu_custom_call" | custom-call | tf_op jit(solution)/shard_map/pallas_call | solution.py:313
  29.7 1.5 %copy.10 = f32[16,1280]{1,0:T(8,128)} copy(f32[16,1280]{1,0:T(8,128)} %shard_map.82) | data formatting | bytes 163840

commit v4 on v3

--- a/solution.py
+++ b/solution.py
@@ -7,7 +7,7 @@
 from jax.sharding import PartitionSpec as P
 
 TILE_TOK = 2
-PIECES = 2
+PIECES = 1
 BANDS = 2
 MESH = pl.DeviceIdType.MESH
 F32 = jnp.float32
@@ -175,7 +175,7 @@
                 pl.semaphore_wait(barrier, expect)
             sib_copy(here).start()
             continue
-        if q == 0 and c == PIECES - 2:
+        if q == 0 and c == 0:
             for q_held, c_held in waiting:
                 send_half((q_held, c_held), gathered((q_held, c_held), local[q_held * PIECES + c_held]))
             waiting = []

time: 31.4 us -> 31 us (0.987)
  Pallas kernels: 29.7 us -> 29.2 us
    pallas_call x1, Pallas kernels: 29.7 us -> 29.2 us  [per_device(): pl.pallas_call(functools.partial(kernel, sizes), out_shape=jax.ShapeDtype...]
where the time goes in v4:
time: 31 us; the launch traced here: 30.8 us
  Pallas kernels  29.2 us (94%)
  local copies, waits for them, and re-layouts  1.53 us (5%)
    pallas_call x1, Pallas kernels, per_device(): pl.pallas_call(functools.partial(kernel, sizes), out_shape=jax.ShapeDtype...  29.2 us
    unnamed x1, local copies, waits for them, and re-layouts  1.53 us

profile of v4, /device:TPU:6, one launch (start us, length us, event | category | flops | bytes accessed | tf_op | source)
XLA Modules:
  0.0 30.8 jit_solution(14647307500929265797)
XLA Ops:
  0.0 29.2 %shard_map.82 = f32[16,1280]{1,0:T(8,128)} custom-call(s32[8]{0:T(128)} %cnt_ref.1, s32[2,8]{1,0:T(2,128)} %bitcast.6, s32[2,8]{1,0:T(2,128)} %bitcast.7, bf16[128,2,256]{2,1,0:T(2,128)(2,1)} %bitcast.5, bf16[512,8192]{1,0:T(8,128)(2,1)} %bitcast.4, bf16[1024,1280]{1,0:T(8,128)(2,1)} %proj_hbm.1, bf16[128,1280]{1,0:T(8,128)(2,1)} %vis_hbm.1, f32[1280]{0:T(1024)} %gain_hbm.1), custom_call_target="tpu_custom_call" | custom-call | tf_op jit(solution)/shard_map/pallas_call | solution.py:313
  29.3 1.5 %copy.10 = f32[16,1280]{1,0:T(8,128)} copy(f32[16,1280]{1,0:T(8,128)} %shard_map.82) | data formatting | bytes 163840

commit v5 on v4

--- a/solution.py
+++ b/solution.py
@@ -9,6 +9,7 @@
 TILE_TOK = 2
 PIECES = 1
 BANDS = 2
+AHEAD = 3
 MESH = pl.DeviceIdType.MESH
 F32 = jnp.float32
 BF16 = jnp.bfloat16
@@ -79,12 +80,12 @@
         cp = pltpu.make_async_copy(
             w_hbm.at[:, pl.ds(pl.multiple_of((block * PIECES + c) * piece, 128), piece)], wbuf.at[i], w_sem.at[i]
         )
-        cp.start()
+        if i < AHEAD:
+            cp.start()
         w_copies[(q, c), sibling] = (i, cp)
     v_copy = pltpu.make_async_copy(vis_hbm.at[pl.ds(pl.multiple_of(g * share, 16), share)], vbuf, v_sem)
     v_copy.start()
     p_copy = pltpu.make_async_copy(proj_hbm, pbuf, p_sem)
-    p_copy.start()
     n_copy = pltpu.make_async_copy(gain_hbm, gain_ref, n_sem)
     n_copy.start()
 
@@ -139,6 +140,10 @@
     def multiply(here, sibling):
         i, cp = w_copies[here, sibling]
         cp.wait()
+        if i + AHEAD < len(order):
+            w_copies[order[i + AHEAD]][1].start()
+        elif i + AHEAD == len(order):
+            p_copy.start()
         return jnp.dot(left, wbuf[i], preferred_element_type=F32)
 
     def sib_copy(here):

time: 31 us -> 29 us (0.935)
  Pallas kernels: 29.2 us -> 27.3 us
    pallas_call x1, Pallas kernels: 29.2 us -> 27.3 us  [per_device(): pl.pallas_call(functools.partial(kernel, sizes), out_shape=jax.ShapeDtype...]
where the time goes in v5:
time: 29 us; the launch traced here: 28.9 us
  Pallas kernels  27.3 us (94%)
  local copies, waits for them, and re-layouts  1.53 us (5%)
    pallas_call x1, Pallas kernels, per_device(): pl.pallas_call(functools.partial(kernel, sizes), out_shape=jax.ShapeDtype...  27.3 us
    unnamed x1, local copies, waits for them, and re-layouts  1.53 us

profile of v5, /device:TPU:6, one launch (start us, length us, event | category | flops | bytes accessed | tf_op | source)
XLA Modules:
  0.0 28.9 jit_solution(7545991512747095588)
XLA Ops:
  0.0 27.3 %shard_map.82 = f32[16,1280]{1,0:T(8,128)} custom-call(s32[8]{0:T(128)} %cnt_ref.1, s32[2,8]{1,0:T(2,128)} %bitcast.6, s32[2,8]{1,0:T(2,128)} %bitcast.7, bf16[128,2,256]{2,1,0:T(2,128)(2,1)} %bitcast.5, bf16[512,8192]{1,0:T(8,128)(2,1)} %bitcast.4, bf16[1024,1280]{1,0:T(8,128)(2,1)} %proj_hbm.1, bf16[128,1280]{1,0:T(8,128)(2,1)} %vis_hbm.1, f32[1280]{0:T(1024)} %gain_hbm.1), custom_call_target="tpu_custom_call" | custom-call | tf_op jit(solution)/shard_map/pallas_call | solution.py:318
  27.3 1.5 %copy.10 = f32[16,1280]{1,0:T(8,128)} copy(f32[16,1280]{1,0:T(8,128)} %shard_map.82) | data formatting | bytes 163840
